TPU v7x, 32 devices: a whole 2x2x4 slice. The times are simulated.
32 devices in a mesh: seq: 16 (over z, y, core), tensor: 2 (over x).
Axes of the slice: x: 2, y: 2, z: 4, core: 2. Of those that a mesh axis runs over, the one named last changes fastest.
Arguments:
- trunk: bfloat16 [2, 1024, 1536], P(None, 'seq', 'tensor'), may hold values from -12 to 12
- w_out: bfloat16 [1536, 1536], P('tensor', 'seq'), may hold values from -1 to 1
- gain_coarse: float32 [1536], replicated, may hold values from 0.1 to 1.9
- w_conv1: bfloat16 [5, 1536, 1536], P(None, 'seq', 'tensor'), may hold values from -0.0625 to 0.0625
- w_up: bfloat16 [1536, 2, 768], P('seq', None, 'tensor'), may hold values from -0.15625 to 0.15625
- skip: bfloat16 [2, 2048, 768], P(None, 'seq', 'tensor'), may hold values from -12 to 12
- gain_fine: float32 [768], replicated, may hold values from 0.1 to 1.9
- w_conv2: bfloat16 [5, 768, 768], P(None, 'seq', 'tensor'), may hold values from -0.09375 to 0.09375
- cotangent: bfloat16 [2, 2048, 768], P(None, 'seq', 'tensor'), may hold values from -6 to 6
Outputs:
- decoded: bfloat16 [2, 2048, 768], P(None, 'seq', 'tensor')
- skip_grad: bfloat16 [2, 2048, 768], P(None, 'seq', 'tensor')
- trunk_grad: bfloat16 [2, 1024, 1536], P(None, 'seq', 'tensor')
All inputs are finite; a program needn't handle non-finite values.
Results may differ from a plain program's by a relative error of at most 0.02.
Values may be sent and summed in bfloat16 or wider, within the bound.
A program may use at most 64 MiB of HBM per device.

v0:
```python
import jax
import jax.numpy as jnp
from jax import lax
from jax.sharding import PartitionSpec as P

C_COARSE = 1536
C_FINE = 768


EPS = 1e-06


def extended(shard, sides, width):
    for axis, dim in sides:
        size, length = (lax.axis_size(axis), shard.shape[dim])
        up = [(i, (i + 1) % size) for i in range(size - 1)]
        down = [(j, i) for i, j in up]
        last = lax.slice_in_dim(shard, length - width, length, axis=dim)
        leading = lax.slice_in_dim(shard, 0, width, axis=dim)
        before = lax.ppermute(last, axis, up)
        after = lax.ppermute(leading, axis, down)
        shard = jnp.concatenate([before, shard, after], axis=dim)
    return shard


def matmul(left, right):
    return lax.dot_general(
        left, right, (((left.ndim - 1,), (0,)), ((), ())), preferred_element_type=jnp.float32
    )


def matmul_back(left, right):
    return lax.dot_general(
        left,
        right,
        (((left.ndim - 1,), (right.ndim - 1,)), ((), ())),
        preferred_element_type=jnp.float32,
    )


def activate(field, gain):
    scaled = field * lax.rsqrt(jnp.mean(field * field, axis=-1, keepdims=True) + EPS)
    return jax.nn.gelu(scaled * gain)


def widen(field):
    return extended(field, (("seq", 1),), 2)


def spread(field):
    return lax.all_gather(field, "tensor", axis=2, tiled=True)


def conv_rows(total, wide, piece):
    length = wide.shape[1] - 4
    for k in range(5):
        total = total + matmul(wide[:, k : k + length], piece[k])
    return total


def conv_back(wide_grad, piece):
    length = wide_grad.shape[1] - 4
    total = jnp.zeros((wide_grad.shape[0], length, piece.shape[1]), jnp.float32)
    for k in range(5):
        total = total + matmul_back(wide_grad[:, 4 - k : 4 - k + length], piece[k])
    return total


def norm_back(partial_grad, field_full, gain, rank, part):
    field = field_full.astype(jnp.float32)
    start = rank * part
    whole = lax.psum(partial_grad.astype(jnp.bfloat16), "tensor").astype(jnp.float32)

    def apply(value):
        return activate(value, gain)

    _, pull = jax.vjp(apply, field)
    return lax.dynamic_slice_in_dim(pull(whole)[0], start, part, 2)


def per_device(trunk, w_out, gain_coarse, w_conv1, w_up, skip, gain_fine, w_conv2, cotangent):
    rank = lax.axis_index("tensor")
    part_coarse = C_COARSE // lax.axis_size("tensor")
    part_fine = C_FINE // lax.axis_size("tensor")
    seqs = trunk.shape[0]
    slab = trunk.shape[1]
    out_w, up_w, conv2_w = (
        lax.all_gather(w_out, "seq", axis=1, tiled=True),
        lax.all_gather(w_up, "seq", axis=0, tiled=True),
        lax.all_gather(w_conv2, "seq", axis=1, tiled=True),
    )
    partial_proj = matmul(trunk, out_w)
    projected = lax.psum_scatter(
        partial_proj.astype(jnp.bfloat16), "tensor", scatter_dimension=2, tiled=True
    )
    projected_full = lax.all_gather(projected, "tensor", axis=2, tiled=True)
    act_coarse = activate(projected_full.astype(jnp.float32), gain_coarse).astype(jnp.bfloat16)
    coarse_wide = widen(act_coarse)
    empty_coarse = jnp.zeros((seqs, slab, part_coarse), jnp.float32)
    mixed_coarse = conv_rows(
        empty_coarse, coarse_wide, lax.all_gather(w_conv1, "seq", axis=1, tiled=True)
    )
    lifted = (projected.astype(jnp.float32) + mixed_coarse).astype(jnp.bfloat16)
    lifted_full = spread(lifted)
    upper = matmul(lifted_full, up_w).reshape(seqs, 2 * slab, part_fine)
    merged = (upper + skip.astype(jnp.float32)).astype(jnp.bfloat16)
    merged_full = spread(merged)
    act_fine = activate(merged_full.astype(jnp.float32), gain_fine).astype(jnp.bfloat16)
    fine_wide = widen(act_fine)
    empty_fine = jnp.zeros((seqs, 2 * slab, part_fine), jnp.float32)
    mixed_fine = conv_rows(empty_fine, fine_wide, conv2_w)
    decoded = (merged.astype(jnp.float32) + mixed_fine).astype(jnp.bfloat16)
    cot_wide = widen(cotangent)
    back_fine = conv_back(cot_wide, conv2_w)
    skip_grad = (
        cotangent.astype(jnp.float32)
        + norm_back(back_fine, merged_full, gain_fine, rank, part_fine)
    ).astype(jnp.bfloat16)
    folded = skip_grad.reshape(seqs, slab, 2 * part_fine)
    up_partial = matmul_back(folded, up_w.reshape(up_w.shape[0], 2 * part_fine))
    lifted_grad = lax.psum_scatter(
        up_partial.astype(jnp.bfloat16), "tensor", scatter_dimension=2, tiled=True
    )
    grad_wide = widen(lifted_grad)
    back_coarse = conv_back(grad_wide, lax.all_gather(w_conv1, "seq", axis=1, tiled=True))
    projected_grad = (
        lifted_grad.astype(jnp.float32)
        + norm_back(back_coarse, projected_full, gain_coarse, rank, part_coarse)
    ).astype(jnp.bfloat16)
    grad_full = spread(projected_grad)
    trunk_grad = matmul_back(grad_full, out_w).astype(jnp.bfloat16)
    return (decoded, skip_grad, trunk_grad)


def solution(mesh):
    in_specs = (
        P(None, "seq", "tensor"),
        P("tensor", "seq"),
        P(),
        P(None, "seq", "tensor"),
        P("seq", None, "tensor"),
        P(None, "seq", "tensor"),
        P(),
        P(None, "seq", "tensor"),
        P(None, "seq", "tensor"),
    )
    out_specs = (P(None, "seq", "tensor"), P(None, "seq", "tensor"), P(None, "seq", "tensor"))
    return jax.shard_map(
        per_device, mesh=mesh, in_specs=in_specs, out_specs=out_specs, check_vma=False
    )
```

profile of v0, /device:TPU:0, one launch (start us, length us, event | category | flops | bytes accessed | tf_op | source)
XLA Modules:
  0.0 373.6 jit_solution(10232408663239553585)
XLA Ops:
  9.6 45.6 %all-gather.5.cloned.1.call-done = bf16[768,1536]{0,1:T(8,128)(2,1)} async-done(((bf16[768,96]{0,1:T(8,128)(2,1)}), bf16[768,1536]{0,1:T(8,128)(2,1)}) %all-gather.5.cloned.1.call-update) | async-done | bytes 2359312 | tf_op jit(solution)/shard_map/all_gather | solution.py:88
  55.3 3.3 convolution_convert_fusion.1
  65.0 34.1 %all-gather.9.cloned.1.call-done = bf16[1536,2,384]{2,0,1:T(8,128)(2,1)} async-done(((bf16[96,2,384]{2,0,1:T(8,128)(2,1)}), bf16[1536,2,384]{2,0,1:T(8,128)(2,1)}) %all-gather.9.cloned.1.call-update) | async-done | bytes 2359312 | tf_op jit(solution)/shard_map/all_gather | solution.py:89
  99.2 2.8 copy.16
  102.0 11.3 %reduce-scatter.3.cloned.1.call-done = bf16[2,64,768]{2,1,0:T(8,128)(2,1)} async-done(((bf16[2,64,1536]{2,1,0:T(8,128)(2,1)}), bf16[2,64,768]{2,1,0:T(8,128)(2,1)}) %reduce-scatter.3.cloned.1.call-update) | async-done | bytes 196624 | tf_op jit(solution)/shard_map/reduce_scatter | solution.py:93
  113.3 7.5 %all_gather.26 = bf16[2,64,1536]{2,1,0:T(8,128)(2,1)S(1)} all-gather(bf16[2,64,768]{2,1,0:T(8,128)(2,1)} %reduce-scatter.3.cloned.1.call-done), channel_id=1, replica_groups=mesh['seq'=16,'tensor'=2] {'tensor'}, dimensions={2}, use_global_device_ids=true | all-gather | bytes 589824 | tf_op jit(solution)/shard_map/all_gather | solution.py:96
  125.1 3.6 collective-permute-start
  128.7 31.9 %all-gather.11.cloned.1.call-done = bf16[5,768,384]{2,1,0:T(8,128)(2,1)} async-done(((bf16[5,48,384]{2,1,0:T(8,128)(2,1)}), bf16[5,768,384]{2,1,0:T(8,128)(2,1)}) %all-gather.11.cloned.1.call-update) | async-done | bytes 2949136 | tf_op jit(solution)/shard_map/all_gather | solution.py:90
  165.7 91.7 %all-gather.7.cloned.1.call-done = bf16[5,1536,768]{2,1,0:T(8,128)(2,1)} async-done(((bf16[5,96,768]{2,1,0:T(8,128)(2,1)}), bf16[5,1536,768]{2,1,0:T(8,128)(2,1)}) %all-gather.7.cloned.1.call-update) | async-done | bytes 11796496 | tf_op jit(solution)/shard_map/all_gather | solution.py:101
  261.8 2.3 fusion.10
  266.3 2.4 fusion.27
  268.7 7.8 %all_gather.28 = bf16[2,64,1536]{2,1,0:T(8,128)(2,1)S(1)} all-gather(bf16[2,64,768]{2,1,0:T(8,128)(2,1)S(1)} %fusion.27), channel_id=1, replica_groups=mesh['seq'=16,'tensor'=2] {'tensor'}, dimensions={2}, use_global_device_ids=true | all-gather | bytes 589824 | tf_op jit(solution)/shard_map/all_gather | solution.py:51
  278.1 9.5 %all_gather.30 = bf16[2,128,768]{2,1,0:T(8,128)(2,1)S(1)} all-gather(bf16[2,128,384]{2,1,0:T(8,128)(2,1)S(1)} %fusion.75), channel_id=1, replica_groups=mesh['seq'=16,'tensor'=2] {'tensor'}, dimensions={2}, use_global_device_ids=true | all-gather | bytes 589824 | tf_op jit(solution)/shard_map/all_gather | solution.py:51
  289.3 2.6 multiply_reduce_fusion.1
  297.5 3.0 collective-permute-start.2
  305.5 3.4 reduce-scatter.5.cloned.1.call-done
  313.0 2.7 fusion.11
  315.7 2.5 fusion.14
  318.3 2.6 fusion.9
  320.9 2.6 fusion.1
  323.5 3.3 fusion.2
  328.9 2.4 fusion.28
  331.3 23.9 %all-reduce.5.cloned.1.call-done = bf16[2,64,1536]{2,1,0:T(8,128)(2,1)} async-done(((bf16[2,64,1536]{2,1,0:T(8,128)(2,1)}), bf16[2,64,1536]{2,1,0:T(8,128)(2,1)}) %all-reduce.5.cloned.1.call-update) | async-done | bytes 393232 | tf_op jit(solution)/shard_map/psum | solution.py:72
  358.3 7.3 %all_gather.32 = bf16[2,64,1536]{2,1,0:T(8,128)(2,1)S(1)} all-gather(bf16[2,64,768]{2,1,0:T(8,128)(2,1)S(1)} %fusion.69), channel_id=1, replica_groups=mesh['seq'=16,'tensor'=2] {'tensor'}, dimensions={2}, use_global_device_ids=true | all-gather | bytes 589824 | tf_op jit(solution)/shard_map/all_gather | solution.py:51
  (102 shorter events, 48.6 us)
Async XLA Ops:
  7.2 48.1 %copy-start = (bf16[2,64,768]{2,1,0:T(8,128)(2,1)S(1)}, bf16[2,64,768]{2,1,0:T(8,128)(2,1)}, u32[]{:S(2)}) copy-start(bf16[2,64,768]{2,1,0:T(8,128)(2,1)} %param.9) | copy-start | bytes 589828
  7.2 52.6 %copy-start.3 = (bf16[2,128,384]{2,1,0:T(8,128)(2,1)S(1)}, bf16[2,128,384]{2,1,0:T(8,128)(2,1)}, u32[]{:S(2)}) copy-start(bf16[2,128,384]{2,1,0:T(8,128)(2,1)} %param.17) | copy-start | bytes 589828
  7.2 48.1 %all-gather.5.cloned.1.call-start = ((), (), s32[]{:S(2)}) async-start(), calls=%async_computation.2 | async-start | bytes 2506752 | tf_op jit(solution)/shard_map/all_gather | solution.py:88
  7.9 91.2 %all-gather.9.cloned.1.call-start = ((), (), s32[]{:S(2)}) async-start(), calls=%async_computation.5 | async-start | bytes 2506752 | tf_op jit(solution)/shard_map/all_gather | solution.py:89
  9.6 103.8 %reduce-scatter.3.cloned.1.call-start = ((), (), s32[]{:S(2)}) async-start(), calls=%async_computation.3 | async-start | bytes 589824 | tf_op jit(solution)/shard_map/reduce_scatter | solution.py:93
  58.6 102.0 %all-gather.11.cloned.1.call-start = ((), (), s32[]{:S(2)}) async-start(), calls=%async_computation.6 | async-start | bytes 3133440 | tf_op jit(solution)/shard_map/all_gather | solution.py:90
  59.2 198.3 %all-gather.7.cloned.1.call-start = ((), (), s32[]{:S(2)}) async-start(), calls=%async_computation.4 | async-start | bytes 12533760 | tf_op jit(solution)/shard_map/all_gather | solution.py:101
  59.7 229.5 %all-reduce.3.cloned.1.call-start = ((), (), s32[]{:S(2)}) async-start(), calls=%async_computation.7 | async-start | bytes 786432 | tf_op jit(solution)/shard_map/psum | solution.py:72
  59.8 68.9 %collective-permute-start.5 = (bf16[2,2,384]{2,1,0:T(2,128)(2,1)S(1)}, bf16[2,2,384]{2,1,0:T(2,128)(2,1)S(1)}, u32[]{:S(2)}, u32[]{:S(2)}) collective-permute-start(bf16[2,2,384]{2,1,0:T(2,128)(2,1)S(1)} %get-tuple-element.15), channel_id=1, source_target_pairs={{0,2},{2,4},{4,6},{6,8},{8,10},{10,12},{12,14},{14,16},{16,18},{18... | collective-permute-start | bytes 9224 | tf_op jit(solution)/shard_map/ppermute | solution.py:20
  62.0 3.1 collective-permute-start.4
  63.3 57.7 %copy-start.12 = (f32[1536]{0:T(1024)S(1)}, f32[1536]{0:T(1024)}, u32[]{:S(2)}) copy-start(f32[1536]{0:T(1024)} %param.11) | copy-start | bytes 18436
  121.0 43.0 %copy-start.13 = (f32[2,64]{1,0:T(2,128)}, f32[2,64]{1,0:T(2,128)S(1)}, u32[]{:S(2)}) copy-start(f32[2,64]{1,0:T(2,128)S(1)} %multiply_reduce_fusion.3) | copy-start | bytes 1540
  123.8 135.8 %collective-permute-start.1 = (bf16[2,2,1536]{2,1,0:T(2,128)(2,1)}, bf16[2,2,1536]{2,1,0:T(2,128)(2,1)}, u32[]{:S(2)}, u32[]{:S(2)}) collective-permute-start(bf16[2,2,1536]{2,1,0:T(2,128)(2,1)} %get-tuple-element.11), channel_id=1, source_target_pairs={{2,0},{4,2},{6,4},{8,6},{10,8},{12,10},{14,12},{16,14},{18,16},{20... | collective-permute-start | bytes 36872 | tf_op jit(solution)/shard_map/ppermute | solution.py:21
  125.1 136.7 %collective-permute-start = (bf16[2,2,1536]{2,1,0:T(2,128)(2,1)}, bf16[2,2,1536]{2,1,0:T(2,128)(2,1)}, u32[]{:S(2)}, u32[]{:S(2)}) collective-permute-start(bf16[2,2,1536]{2,1,0:T(2,128)(2,1)} %get-tuple-element.10), channel_id=1, source_target_pairs={{0,2},{2,4},{4,6},{6,8},{8,10},{10,12},{12,14},{14,16},{16,18},{18... | collective-permute-start | bytes 36872 | tf_op jit(solution)/shard_map/ppermute | solution.py:20
  164.5 93.0 %copy-start.9 = (bf16[2,64,1536]{2,1,0:T(8,128)(2,1)S(1)}, bf16[2,64,1536]{2,1,0:T(8,128)(2,1)}, u32[]{:S(2)}) copy-start(bf16[2,64,1536]{2,1,0:T(8,128)(2,1)} %copy-done.8) | copy-start | bytes 1179652
  165.7 143.3 %reduce-scatter.5.cloned.1.call-start = ((), (), s32[]{:S(2)}) async-start(), calls=%async_computation.8 | async-start | bytes 589824 | tf_op jit(solution)/shard_map/reduce_scatter | solution.py:121
  266.3 10.2 %copy-start.2 = (bf16[1536,2,384]{2,0,1:T(8,128)(2,1)S(1)}, bf16[1536,2,384]{2,0,1:T(8,128)(2,1)}, u32[]{:S(2)}) copy-start(bf16[1536,2,384]{2,0,1:T(8,128)(2,1)} %all-gather.9.cloned.1.call-done) | copy-start | bytes 7077892
  296.1 59.2 %all-reduce.5.cloned.1.call-start = ((), (), s32[]{:S(2)}) async-start(), calls=%async_computation.9 | async-start | bytes 786432 | tf_op jit(solution)/shard_map/psum | solution.py:72
  296.2 30.7 %collective-permute-start.3 = (bf16[2,2,768]{2,1,0:T(2,128)(2,1)S(1)}, bf16[2,2,768]{2,1,0:T(2,128)(2,1)S(1)}, u32[]{:S(2)}, u32[]{:S(2)}) collective-permute-start(bf16[2,2,768]{2,1,0:T(2,128)(2,1)S(1)} %get-tuple-element.9), channel_id=1, source_target_pairs={{2,0},{4,2},{6,4},{8,6},{10,8},{12,10},{14,12},{16,14},{18,16},{20... | collective-permute-start | bytes 18440 | tf_op jit(solution)/shard_map/ppermute | solution.py:21
  297.5 4.5 %collective-permute-start.2 = (bf16[2,2,768]{2,1,0:T(2,128)(2,1)S(1)}, bf16[2,2,768]{2,1,0:T(2,128)(2,1)S(1)}, u32[]{:S(2)}, u32[]{:S(2)}) collective-permute-start(bf16[2,2,768]{2,1,0:T(2,128)(2,1)S(1)} %get-tuple-element.8), channel_id=1, source_target_pairs={{0,2},{2,4},{4,6},{6,8},{8,10},{10,12},{12,14},{14,16},{16,18},{18... | collective-permute-start | bytes 18440 | tf_op jit(solution)/shard_map/ppermute | solution.py:20
  309.8 5.9 %collective-permute-start.7 = (bf16[2,2,768]{2,1,0:T(2,128)(2,1)S(1)}, bf16[2,2,768]{2,1,0:T(2,128)(2,1)S(1)}, u32[]{:S(2)}, u32[]{:S(2)}) collective-permute-start(bf16[2,2,768]{2,1,0:T(2,128)(2,1)S(1)} %get-tuple-element.13), channel_id=1, source_target_pairs={{0,2},{2,4},{4,6},{6,8},{8,10},{10,12},{12,14},{14,16},{16,18},{18... | collective-permute-start | bytes 18440 | tf_op jit(solution)/shard_map/ppermute | solution.py:20
  311.5 6.8 %collective-permute-start.6 = (bf16[2,2,768]{2,1,0:T(2,128)(2,1)S(1)}, bf16[2,2,768]{2,1,0:T(2,128)(2,1)S(1)}, u32[]{:S(2)}, u32[]{:S(2)}) collective-permute-start(bf16[2,2,768]{2,1,0:T(2,128)(2,1)S(1)} %get-tuple-element.12), channel_id=1, source_target_pairs={{2,0},{4,2},{6,4},{8,6},{10,8},{12,10},{14,12},{16,14},{18,16},{20... | collective-permute-start | bytes 18440 | tf_op jit(solution)/shard_map/ppermute | solution.py:21
  326.8 30.3 %copy-start.14 = (f32[2,64]{1,0:T(2,128)S(1)}, f32[2,64]{1,0:T(2,128)}, u32[]{:S(2)}) copy-start(f32[2,64]{1,0:T(2,128)} %copy-done.13) | copy-start | bytes 1540
  328.9 36.7 %copy-start.1 = (bf16[768,1536]{0,1:T(8,128)(2,1)S(1)}, bf16[768,1536]{0,1:T(8,128)(2,1)}, u32[]{:S(2)}) copy-start(bf16[768,1536]{0,1:T(8,128)(2,1)} %all-gather.5.cloned.1.call-done) | copy-start | bytes 7077892
  (8 other events, 27.0 us)
Sparse Core Ops, SparseCore 0:
  10.3 44.9 all-gather.4
  58.1 41.0 all-gather.8
  101.4 11.8 reduce-scatter.2
  115.8 44.7 all-gather.10
  163.0 94.4 all-gather.6
  259.7 26.3 all-reduce.2
  296.2 12.7 reduce-scatter.4
  327.0 28.2 all-reduce.4
where the time goes:
time: 375 us; the launch traced here: 374 us
  waiting for transfers between devices  246 us (66%)
  matrix products  44.9 us (12%)
  blocking collectives  32.2 us (9%)
  starting transfers between devices  16.2 us (4%)
  between operations  14.6 us (4%)
  other arithmetic  10.7 us (3%)
  local copies, waits for them, and re-layouts  9.33 us (2%)
    all_gather x1, waiting for transfers between devices, per_device(): lax.all_gather(w_conv1, 'seq', axis=1, tiled=True)  91.7 us
    all_gather x1, waiting for transfers between devices, per_device(): lax.all_gather(w_out, 'seq', axis=1, tiled=True)  45.6 us
    all_gather x1, waiting for transfers between devices, per_device(): lax.all_gather(w_up, 'seq', axis=0, tiled=True)  34.1 us
    all_gather x1, waiting for transfers between devices, per_device(): lax.all_gather(w_conv2, 'seq', axis=1, tiled=True)  31.9 us
    all_gather x3, blocking collectives, spread(): return lax.all_gather(field, 'tensor', axis=2, tiled=True)  24.7 us
    psum x2, waiting for transfers between devices, norm_back(): lax.psum(partial_grad.astype(jnp.bfloat16), 'tensor').astype(jnp.float32)  23.9 us
    dot_general x12, matrix products, matmul(): lax.dot_general(left, right, (((left.ndim - 1,), (0,)), ((), ())), prefer...  23.8 us
    dot_general x12, matrix products, matmul_back(): lax.dot_general(left, right, (((left.ndim - 1,), (right.ndim - 1,)), ((),...  21.1 us
  transfers between devices with their start and end apart: 16, of which 8 were waited for; matrix products, arithmetic and copies ran while one was open for 14% of the time, Pallas kernels for 0%

commit v1 on v0

--- a/solution.py
+++ b/solution.py
@@ -1,6 +1,10 @@
+import functools
+
 import jax
 import jax.numpy as jnp
 from jax import lax
+from jax.experimental import pallas as pl
+from jax.experimental.pallas import tpu as pltpu
 from jax.sharding import PartitionSpec as P
 
 C_COARSE = 1536
@@ -132,7 +136,500 @@
     return (decoded, skip_grad, trunk_grad)
 
 
+PIECES = 8
+LINE = 4
+HALO = 8
+
+
+def fits(mesh):
+    return mesh.shape["seq"] == 4 * LINE and mesh.shape["tensor"] == 2
+
+
+def gelu_parts(u):
+    c = 0.7978845608028654
+    th = jnp.tanh(c * (u + 0.044715 * (u * u * u)))
+    return 0.5 * (1.0 + th), th, c
+
+
+def gelu(u):
+    half, _, _ = gelu_parts(u)
+    return u * half
+
+
+def gelu_slope(u):
+    half, th, c = gelu_parts(u)
+    return half + 0.5 * u * (1.0 - th * th) * c * (1.0 + 3.0 * 0.044715 * (u * u))
+
+
+def dot(a, b):
+    return jnp.dot(a, b, preferred_element_type=jnp.float32)
+
+
+def dot_t(a, b):
+    return lax.dot_general(a, b, (((1,), (1,)), ((), ())), preferred_element_type=jnp.float32)
+
+
+def fused_kernel(
+    trunk, w_own, w2_own, skip, cot, gain_c, gain_f,
+    decoded, skip_grad, trunk_grad,
+    wb, w2, center, halo, ext, skipf, cotf, pp, pp_in, proj, act, accf, lifted, merged, actf,
+    bf, bf_in, accd, sgf, sgb, ug, ug_in, lgf, lgc, lgk, bc, bc_in, pg,
+    rsem, ssem, lsem, hs, hr, xs, xr,
+):
+    s = lax.axis_index("seq")
+    x = lax.axis_index("tensor")
+    z = s // 4
+    y = (s // 2) % 2
+    c = s % 2
+    rows = ext.shape[0]
+    per = rows // 2
+    slab = per - 2 * HALO
+    half = wb.shape[2]
+    quarter = half // 2
+    seqs = 2
+    MESH = pl.DeviceIdType.MESH
+    bf16 = jnp.bfloat16
+    n_seq = 4 * LINE
+
+    def near(dev):
+        return {"seq": dev}
+
+    ydev = s + 2 - 4 * y
+    cdev = s + 1 - 2 * c
+    xdev = {"tensor": 1 - x}
+
+    own_w = pltpu.make_async_copy(
+        w_own, wb.at[:, pl.ds(pl.multiple_of(s * 96, 96), 96), :], lsem.at[0]
+    )
+    own_w2 = pltpu.make_async_copy(
+        w2_own, w2.at[:, pl.ds(pl.multiple_of(s * 48, 48), 48), :], lsem.at[1]
+    )
+    mine = [pltpu.make_async_copy(r, center.at[i], lsem.at[2 + i]) for i, r in enumerate((trunk, skip, cot))]
+    for copy in [own_w2, own_w] + mine:
+        copy.start()
+
+    barrier = pltpu.get_barrier_semaphore()
+    for dev in (near(ydev), near(cdev), xdev):
+        pl.semaphore_signal(barrier, inc=1, device_id=dev, device_id_type=MESH)
+    for ok, dev in ((z > 0, s - 4), (z < LINE - 1, s + 4), (s > 0, s - 1), (s < n_seq - 1, s + 1)):
+
+        @pl.when(ok)
+        def _(dev=dev):
+            pl.semaphore_signal(barrier, inc=1, device_id=near(dev), device_id_type=MESH)
+
+    one = jnp.int32(1)
+    zero = jnp.int32(0)
+    count = (
+        3
+        + jnp.where(z > 0, one, zero)
+        + jnp.where(z < LINE - 1, one, zero)
+        + jnp.where(s > 0, one, zero)
+        + jnp.where(s < n_seq - 1, one, zero)
+    )
+    pl.semaphore_wait(barrier, count)
+
+    def halo_copy(i, side, dev):
+        lo = slab - 16 if side == 0 else 0
+        return pltpu.make_async_remote_copy(
+            src_ref=center.at[i, :, pl.ds(lo, 16), :],
+            dst_ref=halo.at[i, side],
+            send_sem=hs.at[i, side],
+            recv_sem=hr.at[i, side],
+            device_id=near(dev),
+            device_id_type=MESH,
+        )
+
+    def ref(p, owner, wide):
+        if wide:
+            return w2.at[:, pl.ds(pl.multiple_of(owner * 48, 48), 48), :]
+        return wb.at[p - 1, pl.ds(pl.multiple_of(owner * 96, 96), 96), :]
+
+    def send(p, owner, wide, way, dev):
+        return pltpu.make_async_remote_copy(
+            src_ref=ref(p, owner, wide),
+            dst_ref=ref(p, owner, wide),
+            send_sem=ssem.at[p, owner, way],
+            recv_sem=rsem.at[p, owner],
+            device_id=near(dev),
+            device_id_type=MESH,
+        )
+
+    def routes():
+        out = []
+        for d in range(LINE):
+            for sign in (1, -1) if d else (0,):
+                out.append((d, sign, False))
+                out.append((d, sign, True))
+        return out
+
+    def each(p, d, sign, across, act_on):
+        zz = z - sign * d
+        base = s - 4 * sign * d
+        owner = base + 2 - 4 * y if across else base
+        there = (zz >= 0) & (zz < LINE) & (p >= 0) & (p < PIECES)
+        for wide in (True, False):
+
+            @pl.when(there & ((p == 0) if wide else (p > 0)))
+            def _(wide=wide):
+                act_on(p, owner, wide, d, sign, across)
+
+    def targets(p, owner, wide, sign, across, do):
+        if not across:
+            if sign >= 0:
+
+                @pl.when(z < LINE - 1)
+                def _():
+                    do(send(p, owner, wide, 0, s + 4))
+
+            if sign <= 0:
+
+                @pl.when(z > 0)
+                def _():
+                    do(send(p, owner, wide, 1, s - 4))
+
+            do(send(p, owner, wide, 2, ydev))
+        do(send(p, owner, wide, 3, cdev))
+
+    def forward(p, owner, wide, d, sign, across):
+        if d or across:
+            send(p, owner, wide, 3, cdev).wait_recv()
+        targets(p, owner, wide, sign, across, lambda copy: copy.start())
+
+    def drain(p, owner, wide, d, sign, across):
+        targets(p, owner, wide, sign, across, lambda copy: copy.wait_send())
+
+    def step(t):
+        for d, sign, across in routes():
+            each(t - d - (1 if across else 0), d, sign, across, forward)
+
+    def from_core(p, wide):
+        def body(i, carry):
+            owner = 2 * i + 1 - c
+            send(p, owner, wide, 3, cdev).wait_recv()
+            return carry
+
+        lax.fori_loop(0, 2 * LINE, body, 0)
+
+    def exchange(i, src, dst):
+        return pltpu.make_async_remote_copy(
+            src_ref=src,
+            dst_ref=dst,
+            send_sem=xs.at[i],
+            recv_sem=xr.at[i],
+            device_id=xdev,
+            device_id_type=MESH,
+        )
+
+    def loop(n, body):
+        def run(i, carry):
+            body(i)
+            return carry
+
+        lax.fori_loop(0, n, run, 0)
+
+    own_w2.wait()
+    own_w.wait()
+    for copy in mine:
+        copy.wait()
+    for i in range(3):
+        for side, ok, dev in ((0, s < n_seq - 1, s + 1), (1, s > 0, s - 1)):
+
+            @pl.when(ok)
+            def _(i=i, side=side, dev=dev):
+                halo_copy(i, side, dev).start()
+
+    loop(4, step)
+
+    for i in range(3):
+        for side, ok in ((0, s > 0), (1, s < n_seq - 1)):
+
+            @pl.when(ok)
+            def _(i=i, side=side):
+                halo_copy(i, side, cdev).wait_recv()
+
+            @pl.when(jnp.logical_not(ok))
+            def _(i=i, side=side):
+                halo[i, side] = jnp.zeros(halo.shape[2:], bf16)
+
+    for i in range(3):
+        for q in range(seqs):
+            before = halo[i, 0, q].astype(jnp.float32)[16 - HALO :]
+            after = halo[i, 1, q].astype(jnp.float32)[:HALO]
+            whole = jnp.concatenate([before, center[i, q].astype(jnp.float32), after], axis=0)
+            if i == 0:
+                ext[pl.ds(q * per, per), :] = whole.astype(bf16)
+            elif i == 1:
+                skipf[pl.ds(q * per, per), :] = whole
+            else:
+                cotf[pl.ds(q * per, per), :] = whole
+
+    def inside(start, size):
+        r = start + lax.broadcasted_iota(jnp.int32, (size, 1), 0)
+        at = jnp.where(r >= per, r - per, r) + s * slab - HALO
+        return (at >= 0) & (at < n_seq * slab)
+
+    lax.fori_loop(4, 6, lambda t, k: (step(t), k)[1], 0)
+    from_core(0, True)
+    from_core(1, False)
+
+    def project(n):
+        cols = pl.ds(pl.multiple_of(n * 256, 256), 256)
+        pp[:, cols] = dot_t(ext[...], wb[0, cols, :]).astype(bf16)
+
+    loop(2 * half // 256, project)
+    send_pp = exchange(0, pp, pp_in)
+    send_pp.start()
+
+    step(6)
+
+    def roll(v, shift):
+        return pltpu.roll(v, shift % rows, 0)
+
+    c0 = cotf[:, :quarter]
+    c1 = cotf[:, quarter:]
+    b0, b1 = c0.astype(bf16), c1.astype(bf16)
+    up0, up1 = roll(c0, -1).astype(bf16), roll(c1, -1).astype(bf16)
+    dn0, dn1 = roll(c0, 1).astype(bf16), roll(c1, 1).astype(bf16)
+    even = (up0, b1, b0, dn1, dn0)
+    odd = (up1, up0, b1, b0, dn1)
+
+    def back_fine(n):
+        cols = pl.ds(pl.multiple_of(n * 256, 256), 256)
+        for par, taps in ((0, even), (1, odd)):
+            total = dot_t(taps[0], w2[0, cols, :])
+            for k in range(1, 5):
+                total = total + dot_t(taps[k], w2[k, cols, :])
+            bf[par, :, cols] = total.astype(bf16)
+
+    loop(half // 256, back_fine)
+    send_bf = exchange(1, bf, bf_in)
+    send_bf.start()
+
+    send_pp.wait_recv()
+
+    def norm(f):
+        return lax.rsqrt(jnp.mean(f * f, axis=-1, keepdims=True) + EPS)
+
+    def coarse(i):
+        at = pl.ds(pl.multiple_of(i * 32, 32), 32)
+        f = (pp[at, :].astype(jnp.float32) + pp_in[at, :].astype(jnp.float32)).astype(bf16).astype(jnp.float32)
+        proj[at, :] = f
+        a = gelu(f * norm(f) * gain_c[...])
+        act[at, :] = jnp.where(inside(i * 32, 32), a, 0.0).astype(bf16)
+
+    loop(rows // 32, coarse)
+    xhalf = pl.ds(pl.multiple_of(x * half, half), half)
+    accf[...] = proj[:, xhalf]
+
+    def tap_ahead(k):
+        step(7 + k)
+        from_core(3 + k, False)
+        for n in range(half // 256):
+            cols = pl.ds(n * 256, 256)
+            accf[:, cols] += pltpu.roll(dot(act[...], wb[2 + k, :, cols]), lax.rem(rows + 2 - k, rows), 0)
+
+    loop(5, tap_ahead)
+    lifted[:, xhalf] = accf[...].astype(bf16)
+    send_lifted = exchange(2, lifted.at[:, xhalf], lifted.at[:, xhalf])
+    send_lifted.start()
+    from_core(2, False)
+    exchange(2, lifted.at[:, pl.ds(pl.multiple_of((1 - x) * half, half), half)], lifted.at[:, pl.ds(pl.multiple_of((1 - x) * half, half), half)]).wait_recv()
+    xq = pl.ds(pl.multiple_of(x * quarter, quarter), quarter)
+    oq = pl.ds(pl.multiple_of((1 - x) * quarter, quarter), quarter)
+    for n in range(half // 384):
+        cols = pl.ds(n * 384, 384)
+        m = (dot(lifted[...], wb[1, :, cols]) + skipf[:, cols]).astype(bf16)
+        merged[n, :, xq] = m
+        accd[:, cols] = m.astype(jnp.float32)
+    send_merged = exchange(3, merged.at[:, :, xq], merged.at[:, :, xq])
+    send_merged.start()
+    send_bf.wait_recv()
+    exchange(3, merged.at[:, :, oq], merged.at[:, :, oq]).wait_recv()
+
+    def pull(f, gain, grad):
+        r = norm(f)
+        dn = grad * gelu_slope(f * r * gain) * gain
+        return r * dn - f * (r * r * r * jnp.mean(dn * f, axis=-1, keepdims=True))
+
+    def fine(i):
+        at = pl.ds(pl.multiple_of(i * 32, 32), 32)
+        for par in range(2):
+            f = merged[par, at, :].astype(jnp.float32)
+            u = f * norm(f) * gain_f[...]
+            actf[par, at, :] = jnp.where(inside(i * 32, 32), gelu(u), 0.0).astype(bf16)
+            g = bf[par, at, :].astype(jnp.float32) + bf_in[par, at, :].astype(jnp.float32)
+            df = pull(f, gain_f[...], g)
+            mine = jnp.where(x == 0, df[:, :quarter], df[:, quarter:])
+            cols = pl.ds(par * quarter, quarter)
+            v = cotf[at, cols] + mine
+            sgf[at, cols] = v
+            sgb[at, cols] = v.astype(bf16)
+
+    loop(rows // 32, fine)
+
+    def up_back(which, out):
+        def body(n):
+            cols = pl.ds(pl.multiple_of(n * 256, 256), 256)
+            wrow = pl.ds(pl.multiple_of(which * half + n * 256, 256), 256)
+            out[:, cols] = dot_t(sgb[...], wb[1, wrow, :]).astype(bf16)
+
+        loop(half // 256, body)
+
+    up_back(1 - x, ug)
+    send_ug = exchange(4, ug, ug_in)
+    send_ug.start()
+    send_lifted.wait_send()
+    up_back(x, lifted.at[:, pl.ds(0, half)])
+    for q in range(seqs):
+        skip_grad[q] = sgf[pl.ds(q * per + HALO, slab), :].astype(bf16)
+    send_ug.wait_recv()
+
+    def meet(i):
+        at = pl.ds(pl.multiple_of(i * 32, 32), 32)
+        v = lifted[at, :half].astype(jnp.float32) + ug_in[at, :].astype(jnp.float32)
+        lgf[at, :] = jnp.where(inside(i * 32, 32), v, 0.0).astype(bf16).astype(jnp.float32)
+
+    loop(rows // 32, meet)
+    for q in range(seqs):
+        lgc[pl.ds(q * slab, slab), xhalf] = lgf[pl.ds(q * per + HALO, slab), :].astype(bf16)
+    send_lg = exchange(5, lgc.at[:, xhalf], lgc.at[:, xhalf])
+    send_lg.start()
+
+    def shifted(k):
+        v = pltpu.roll(lgf[...], lax.rem(rows + k - 2, rows), 0)
+        for q in range(seqs):
+            lgk[k, pl.ds(q * slab, slab), :] = v[q * per + HALO : q * per + HALO + slab].astype(bf16)
+
+    loop(5, shifted)
+
+    def back_coarse(n):
+        cols = pl.ds(pl.multiple_of(n * 256, 256), 256)
+        total = dot_t(lgk[0], wb[2, cols, :])
+        for k in range(1, 5):
+            total = total + dot_t(lgk[k], wb[2 + k, cols, :])
+        bc[:, cols] = total.astype(bf16)
+
+    loop(2 * half // 256, back_coarse)
+    send_bc = exchange(6, bc, bc_in)
+    send_bc.start()
+
+    e = {}
+    for k in range(5):
+        e[k] = [dot(actf[par], w2[k]) for par in range(2)]
+        for par in range(2):
+            fine_at = par - (k - 2)
+            q = fine_at % 2
+            shift = (fine_at - q) // 2
+            v = e[k][par] if shift == 0 else roll(e[k][par], shift)
+            accd[:, q * quarter : (q + 1) * quarter] += v
+    for q in range(seqs):
+        decoded[q] = accd[pl.ds(q * per + HALO, slab), :].astype(bf16)
+
+    oth = pl.ds(pl.multiple_of((1 - x) * half, half), half)
+    exchange(5, lgc.at[:, oth], lgc.at[:, oth]).wait_recv()
+    send_bc.wait_recv()
+    for q in range(seqs):
+
+        def last(i, q=q):
+            at = pl.ds(pl.multiple_of(q * slab + i * 32, 32), 32)
+            f = proj[pl.ds(pl.multiple_of(q * per + HALO + i * 32, 8), 32), :]
+            g = bc[at, :].astype(jnp.float32) + bc_in[at, :].astype(jnp.float32)
+            pg[at, :] = (lgc[at, :].astype(jnp.float32) + pull(f, gain_c[...], g)).astype(bf16)
+
+        loop(slab // 32, last)
+    for n in range(half // 256):
+        cols = pl.ds(n * 256, 256)
+        v = dot(pg[...], wb[0, :, cols]).astype(bf16)
+        for q in range(seqs):
+            trunk_grad[q, :, cols] = v[q * slab : (q + 1) * slab]
+
+    for copy in (send_pp, send_bf, send_merged, send_ug, send_lg, send_bc):
+        copy.wait_send()
+    for i in range(3):
+        for side, ok, dev in ((0, s < n_seq - 1, s + 1), (1, s > 0, s - 1)):
+
+            @pl.when(ok)
+            def _(i=i, side=side, dev=dev):
+                halo_copy(i, side, dev).wait_send()
+
+    def finish(p):
+        for d, sign, across in routes():
+            each(p, d, sign, across, drain)
+
+    loop(PIECES, finish)
+
+
+def per_device_fused(trunk, w_out, gain_coarse, w_conv1, w_up, skip, gain_fine, w_conv2, cotangent):
+    seqs, slab, half = trunk.shape
+    quarter = half // 2
+    n = lax.axis_size("seq")
+    rows = seqs * (slab + 2 * HALO)
+    w_own = jnp.concatenate([w_out.T[None], w_up.reshape(1, -1, half), w_conv1], axis=0)
+    bf16, f32 = jnp.bfloat16, jnp.float32
+    V = pltpu.VMEM
+    out = jax.ShapeDtypeStruct((seqs, slab, half), bf16)
+    vm = pl.BlockSpec(memory_space=pltpu.VMEM)
+    anyw = pl.BlockSpec(memory_space=pl.ANY)
+    decoded, skip_grad, trunk_grad = pl.pallas_call(
+        fused_kernel,
+        out_shape=(out, out, out),
+        in_specs=[anyw] * 5 + [vm] * 2,
+        out_specs=(vm, vm, vm),
+        scratch_shapes=[
+            V((7, 2 * half, half), bf16),
+            V((5, half, quarter), bf16),
+            V((3, seqs, slab, half), bf16),
+            V((3, 2, seqs, 16, half), bf16),
+            V((rows, half), bf16),
+            V((rows, half), f32),
+            V((rows, half), f32),
+            V((rows, 2 * half), bf16),
+            V((rows, 2 * half), bf16),
+            V((rows, 2 * half), f32),
+            V((rows, 2 * half), bf16),
+            V((rows, half), f32),
+            V((rows, 2 * half), bf16),
+            V((2, rows, half), bf16),
+            V((2, rows, half), bf16),
+            V((2, rows, half), bf16),
+            V((2, rows, half), bf16),
+            V((rows, half), f32),
+            V((rows, half), f32),
+            V((rows, half), bf16),
+            V((rows, half), bf16),
+            V((rows, half), bf16),
+            V((rows, half), f32),
+            V((seqs * slab, 2 * half), bf16),
+            V((5, seqs * slab, half), bf16),
+            V((seqs * slab, 2 * half), bf16),
+            V((seqs * slab, 2 * half), bf16),
+            V((seqs * slab, 2 * half), bf16),
+            pltpu.SemaphoreType.DMA((PIECES, n)),
+            pltpu.SemaphoreType.DMA((PIECES, n, 4)),
+            pltpu.SemaphoreType.DMA((5,)),
+            pltpu.SemaphoreType.DMA((3, 2)),
+            pltpu.SemaphoreType.DMA((3, 2)),
+            pltpu.SemaphoreType.DMA((7,)),
+            pltpu.SemaphoreType.DMA((7,)),
+        ],
+        compiler_params=pltpu.CompilerParams(
+            collective_id=0, has_side_effects=True, vmem_limit_bytes=56 * 1024 * 1024
+        ),
+    )(
+        trunk,
+        w_own,
+        w_conv2,
+        skip.reshape(seqs, slab, half),
+        cotangent.reshape(seqs, slab, half),
+        gain_coarse.reshape(1, -1),
+        gain_fine.reshape(1, -1),
+    )
+    wide = (seqs, 2 * slab, quarter)
+    return decoded.reshape(wide), skip_grad.reshape(wide), trunk_grad
+
+
 def solution(mesh):
+    body = per_device_fused if fits(mesh) else per_device
     in_specs = (
         P(None, "seq", "tensor"),
         P("tensor", "seq"),
@@ -146,5 +643,5 @@
     )
     out_specs = (P(None, "seq", "tensor"), P(None, "seq", "tensor"), P(None, "seq", "tensor"))
     return jax.shard_map(
-        per_device, mesh=mesh, in_specs=in_specs, out_specs=out_specs, check_vma=False
-    )
+        body, mesh=mesh, in_specs=in_specs, out_specs=out_specs, check_vma=False
+    )

time: 375 us -> 180 us (0.48)
  waiting for transfers between devices: 246 us -> 0 us
  Pallas kernels: 0 us -> 168 us
  matrix products: 44.9 us -> 0 us
  blocking collectives: 32.2 us -> 0 us
  starting transfers between devices: 16.2 us -> 0 us
  between operations: 14.6 us -> 0.68 us
  other arithmetic: 10.7 us -> 1.05 us
    all_gather x4 -> x0, waiting for transfers between devices: 203 us -> none  [the longest x1 91.7 us: per_device(): lax.all_gather(w_conv1, 'seq', axis=1, tiled=True)]
    pallas_call x0 -> x1, Pallas kernels: none -> 168 us  [per_device_fused(): pl.pallas_call(fused_kernel, out_shape=(out, out, out), in_specs=[anyw] *...]
    dot_general x24 -> x0, matrix products: 44.9 us -> none  [the longest x12 23.8 us: matmul(): lax.dot_general(left, right, (((left.ndim - 1,), (0,)), ((), ())), prefer...]
    all_gather x4 -> x0, blocking collectives: 32.2 us -> none  [the longest x3 24.7 us: spread(): return lax.all_gather(field, 'tensor', axis=2, tiled=True)]
    psum x2 -> x0, waiting for transfers between devices: 23.9 us -> none  [norm_back(): lax.psum(partial_grad.astype(jnp.bfloat16), 'tensor').astype(jnp.float32)]
    ppermute x8 -> x0, starting transfers between devices: 15.9 us -> none  [the longest x4 10.5 us: extended(): before = lax.ppermute(last, axis, up)]
    reduce_scatter x2 -> x0, waiting for transfers between devices: 14.8 us -> none  [the longest x1 11.3 us: per_device(): lax.psum_scatter(partial_proj.astype(jnp.bfloat16), 'tensor', scatter_dim...]
    reshape x1 -> x7, local copies, waits for them, and re-layouts: 0.99 us -> 8.56 us  [the longest x2 2.46 us: per_device_fused(): return (decoded.reshape(wide), skip_grad.reshape(wide), trunk_grad)]
  transfers between devices with their start and end apart: 16 -> 0, of which waited for: 8 -> 0; matrix products, arithmetic and copies ran while one was open for 14% -> 0% of each run, Pallas kernels for 0% -> 0%
where the time goes in v1:
time: 180 us; the launch traced here: 179 us
  Pallas kernels  168 us (93%)
  local copies, waits for them, and re-layouts  9.46 us (5%)
    pallas_call x1, Pallas kernels, per_device_fused(): pl.pallas_call(fused_kernel, out_shape=(out, out, out), in_specs=[anyw] *...  168 us

profile of v1, /device:TPU:0, one launch (start us, length us, event | category | flops | bytes accessed | tf_op | source)
XLA Modules:
  0.0 179.4 jit_solution(10703120053971760330)
XLA Ops:
  0.6 0.0 copy-start.1
  0.6 0.0 copy-start
  0.7 1.4 reshape.31.gain_f
  2.0 1.3 reshape.30.gain_c
  3.3 1.0 reshape.27
  4.3 0.0 copy-done.1
  4.3 0.7 reshape.28.skip
  5.1 0.0 copy-start.4
  5.1 1.7 reshape.29.cot
  6.8 0.0 copy-done
  6.8 0.0 copy-done.4
  6.8 1.0 pad_maximum_fusion.w_own
  7.8 168.2 %shard_map.112 = (bf16[2,64,768]{2,1,0:T(8,128)(2,1)}, bf16[2,64,768]{2,1,0:T(8,128)(2,1)}, bf16[2,64,768]{2,1,0:T(8,128)(2,1)}) custom-call(bf16[2,64,768]{2,1,0:T(8,128)(2,1)} %trunk.1, bf16[7,96,768]{2,1,0:T(8,128)(2,1)} %pad_maximum_fusion.w_own, bf16[5,48,384]{2,1,0:T(8,128)(2,1)} %w2_own.1, bf16[2,64,768]{2,1,0:T(8,128)(2,1)} %reshape.28.skip, ...), custom_call_target="tpu_custom_call" | custom-call | tf_op jit(solution)/shard_map/pallas_call | solution.py:573
  176.0 0.0 copy-start.3
  176.0 1.7 reshape.32
  177.8 0.0 copy-done.3
  177.8 0.0 copy-start.2
  177.8 0.7 reshape.33
  178.5 0.2 copy-done.2
  178.7 0.7 copy.13
Async XLA Ops:
  0.6 3.7 %copy-start.1 = (bf16[2,128,384]{2,1,0:T(8,128)(2,1)S(1)}, bf16[2,128,384]{2,1,0:T(8,128)(2,1)}, u32[]{:S(2)}) copy-start(bf16[2,128,384]{2,1,0:T(8,128)(2,1)} %param.14) | copy-start | bytes 589828
  0.6 6.1 %copy-start = (bf16[5,96,768]{2,1,0:T(8,128)(2,1)S(1)}, bf16[5,96,768]{2,1,0:T(8,128)(2,1)}, u32[]{:S(2)}) copy-start(bf16[5,96,768]{2,1,0:T(8,128)(2,1)} %param.12) | copy-start | bytes 2211844
  5.1 1.7 copy-start.4
  176.0 1.7 copy-start.3
  177.8 1.0 copy-start.2

commit v2 on v1

--- a/solution.py
+++ b/solution.py
@@ -137,6 +137,7 @@
 
 
 PIECES = 8
+Y_FIRST = 3
 LINE = 4
 HALO = 8
 
@@ -187,6 +188,7 @@
     half = wb.shape[2]
     quarter = half // 2
     seqs = 2
+    gain_c, gain_f = gain_c[...].reshape(1, -1), gain_f[...].reshape(1, -1)
     MESH = pl.DeviceIdType.MESH
     bf16 = jnp.bfloat16
     n_seq = 4 * LINE
@@ -273,8 +275,10 @@
             def _(wide=wide):
                 act_on(p, owner, wide, d, sign, across)
 
-    def targets(p, owner, wide, sign, across, do):
-        if not across:
+    def targets(p, owner, wide, d, sign, across, do):
+        first = False if wide else p == Y_FIRST
+
+        def along():
             if sign >= 0:
 
                 @pl.when(z < LINE - 1)
@@ -287,16 +291,28 @@
                 def _():
                     do(send(p, owner, wide, 1, s - 4))
 
-            do(send(p, owner, wide, 2, ydev))
+        if across:
+            if not wide:
+                pl.when(first)(along)
+        else:
+            along()
+            if d == 0 or wide:
+                do(send(p, owner, wide, 2, ydev))
+            else:
+
+                @pl.when(jnp.logical_not(first))
+                def _():
+                    do(send(p, owner, wide, 2, ydev))
+
         do(send(p, owner, wide, 3, cdev))
 
     def forward(p, owner, wide, d, sign, across):
         if d or across:
             send(p, owner, wide, 3, cdev).wait_recv()
-        targets(p, owner, wide, sign, across, lambda copy: copy.start())
+        targets(p, owner, wide, d, sign, across, lambda copy: copy.start())
 
     def drain(p, owner, wide, d, sign, across):
-        targets(p, owner, wide, sign, across, lambda copy: copy.wait_send())
+        targets(p, owner, wide, d, sign, across, lambda copy: copy.wait_send())
 
     def step(t):
         for d, sign, across in routes():
@@ -380,7 +396,7 @@
     send_pp = exchange(0, pp, pp_in)
     send_pp.start()
 
-    step(6)
+    step(jnp.int32(6))
 
     def roll(v, shift):
         return pltpu.roll(v, shift % rows, 0)
@@ -414,7 +430,7 @@
         at = pl.ds(pl.multiple_of(i * 32, 32), 32)
         f = (pp[at, :].astype(jnp.float32) + pp_in[at, :].astype(jnp.float32)).astype(bf16).astype(jnp.float32)
         proj[at, :] = f
-        a = gelu(f * norm(f) * gain_c[...])
+        a = gelu(f * norm(f) * gain_c)
         act[at, :] = jnp.where(inside(i * 32, 32), a, 0.0).astype(bf16)
 
     loop(rows // 32, coarse)
@@ -422,23 +438,28 @@
     accf[...] = proj[:, xhalf]
 
     def tap_ahead(k):
-        step(7 + k)
-        from_core(3 + k, False)
+        from_core(2 + k, False)
         for n in range(half // 256):
             cols = pl.ds(n * 256, 256)
-            accf[:, cols] += pltpu.roll(dot(act[...], wb[2 + k, :, cols]), lax.rem(rows + 2 - k, rows), 0)
-
-    loop(5, tap_ahead)
+            accf[:, cols] += pltpu.roll(dot(act[...], wb[1 + k, :, cols]), lax.rem(rows + 2 - k, rows), 0)
+
+    def tap_and_step(k):
+        step(7 + k)
+        tap_ahead(k)
+
+    loop(4, tap_and_step)
+    tap_ahead(jnp.int32(4))
     lifted[:, xhalf] = accf[...].astype(bf16)
     send_lifted = exchange(2, lifted.at[:, xhalf], lifted.at[:, xhalf])
     send_lifted.start()
-    from_core(2, False)
+    step(jnp.int32(11))
+    from_core(7, False)
     exchange(2, lifted.at[:, pl.ds(pl.multiple_of((1 - x) * half, half), half)], lifted.at[:, pl.ds(pl.multiple_of((1 - x) * half, half), half)]).wait_recv()
     xq = pl.ds(pl.multiple_of(x * quarter, quarter), quarter)
     oq = pl.ds(pl.multiple_of((1 - x) * quarter, quarter), quarter)
     for n in range(half // 384):
         cols = pl.ds(n * 384, 384)
-        m = (dot(lifted[...], wb[1, :, cols]) + skipf[:, cols]).astype(bf16)
+        m = (dot(lifted[...], wb[6, :, cols]) + skipf[:, cols]).astype(bf16)
         merged[n, :, xq] = m
         accd[:, cols] = m.astype(jnp.float32)
     send_merged = exchange(3, merged.at[:, :, xq], merged.at[:, :, xq])
@@ -455,10 +476,10 @@
         at = pl.ds(pl.multiple_of(i * 32, 32), 32)
         for par in range(2):
             f = merged[par, at, :].astype(jnp.float32)
-            u = f * norm(f) * gain_f[...]
+            u = f * norm(f) * gain_f
             actf[par, at, :] = jnp.where(inside(i * 32, 32), gelu(u), 0.0).astype(bf16)
             g = bf[par, at, :].astype(jnp.float32) + bf_in[par, at, :].astype(jnp.float32)
-            df = pull(f, gain_f[...], g)
+            df = pull(f, gain_f, g)
             mine = jnp.where(x == 0, df[:, :quarter], df[:, quarter:])
             cols = pl.ds(par * quarter, quarter)
             v = cotf[at, cols] + mine
@@ -471,7 +492,7 @@
         def body(n):
             cols = pl.ds(pl.multiple_of(n * 256, 256), 256)
             wrow = pl.ds(pl.multiple_of(which * half + n * 256, 256), 256)
-            out[:, cols] = dot_t(sgb[...], wb[1, wrow, :]).astype(bf16)
+            out[:, cols] = dot_t(sgb[...], wb[6, wrow, :]).astype(bf16)
 
         loop(half // 256, body)
 
@@ -504,9 +525,9 @@
 
     def back_coarse(n):
         cols = pl.ds(pl.multiple_of(n * 256, 256), 256)
-        total = dot_t(lgk[0], wb[2, cols, :])
+        total = dot_t(lgk[0], wb[1, cols, :])
         for k in range(1, 5):
-            total = total + dot_t(lgk[k], wb[2 + k, cols, :])
+            total = total + dot_t(lgk[k], wb[1 + k, cols, :])
         bc[:, cols] = total.astype(bf16)
 
     loop(2 * half // 256, back_coarse)
@@ -534,7 +555,7 @@
             at = pl.ds(pl.multiple_of(q * slab + i * 32, 32), 32)
             f = proj[pl.ds(pl.multiple_of(q * per + HALO + i * 32, 8), 32), :]
             g = bc[at, :].astype(jnp.float32) + bc_in[at, :].astype(jnp.float32)
-            pg[at, :] = (lgc[at, :].astype(jnp.float32) + pull(f, gain_c[...], g)).astype(bf16)
+            pg[at, :] = (lgc[at, :].astype(jnp.float32) + pull(f, gain_c, g)).astype(bf16)
 
         loop(slab // 32, last)
     for n in range(half // 256):
@@ -564,7 +585,7 @@
     quarter = half // 2
     n = lax.axis_size("seq")
     rows = seqs * (slab + 2 * HALO)
-    w_own = jnp.concatenate([w_out.T[None], w_up.reshape(1, -1, half), w_conv1], axis=0)
+    w_own = jnp.concatenate([w_out.T[None], w_conv1, w_up.reshape(1, -1, half)], axis=0)
     bf16, f32 = jnp.bfloat16, jnp.float32
     V = pltpu.VMEM
     out = jax.ShapeDtypeStruct((seqs, slab, half), bf16)
@@ -621,8 +642,8 @@
         w_conv2,
         skip.reshape(seqs, slab, half),
         cotangent.reshape(seqs, slab, half),
-        gain_coarse.reshape(1, -1),
-        gain_fine.reshape(1, -1),
+        gain_coarse,
+        gain_fine,
     )
     wide = (seqs, 2 * slab, quarter)
     return decoded.reshape(wide), skip_grad.reshape(wide), trunk_grad

time: 180 us -> 164 us (0.911)
  Pallas kernels: 168 us -> 155 us
  local copies, waits for them, and re-layouts: 9.46 us -> 6.89 us
    pallas_call x1, Pallas kernels: 168 us -> 155 us  [per_device_fused(): pl.pallas_call(fused_kernel, out_shape=(out, out, out), in_specs=[anyw] *...]
    reshape x2 -> x0, local copies, waits for them, and re-layouts: 2.65 us -> none  [the longest x1 1.35 us: per_device_fused(): gain_fine.reshape(1, -1)]
where the time goes in v2:
time: 164 us; the launch traced here: 163 us
  Pallas kernels  155 us (95%)
  local copies, waits for them, and re-layouts  6.89 us (4%)
    pallas_call x1, Pallas kernels, per_device_fused(): pl.pallas_call(fused_kernel, out_shape=(out, out, out), in_specs=[anyw] *...  155 us

profile of v2, /device:TPU:0, one launch (start us, length us, event | category | flops | bytes accessed | tf_op | source)
XLA Modules:
  0.0 163.3 jit_solution(10364854216537922154)
XLA Ops:
  0.6 0.0 copy-start.1
  0.6 0.0 copy-start
  0.7 1.1 reshape.21
  1.7 0.0 copy-done.1
  1.7 0.7 reshape.22.skip
  2.5 0.0 copy-start.4
  2.5 1.7 %reshape.23.cot = bf16[2,64,768]{2,1,0:T(8,128)(2,1)} reshape(bf16[2,128,384]{2,1,0:T(8,128)(2,1)} %param.17) | data formatting | bytes 393216 | tf_op jit(solution)/shard_map/reshape | solution.py:644
  4.2 0.0 copy-done
  4.2 0.0 copy-done.4
  4.2 1.1 pad_maximum_fusion.w_own
  5.3 154.7 %shard_map.112 = (bf16[2,64,768]{2,1,0:T(8,128)(2,1)}, bf16[2,64,768]{2,1,0:T(8,128)(2,1)}, bf16[2,64,768]{2,1,0:T(8,128)(2,1)}) custom-call(bf16[2,64,768]{2,1,0:T(8,128)(2,1)} %trunk.1, bf16[7,96,768]{2,1,0:T(8,128)(2,1)} %pad_maximum_fusion.w_own, bf16[5,48,384]{2,1,0:T(8,128)(2,1)} %w2_own.1, bf16[2,64,768]{2,1,0:T(8,128)(2,1)} %reshape.22.skip, ...), custom_call_target="tpu_custom_call" | custom-call | tf_op jit(solution)/shard_map/pallas_call | solution.py:594
  160.0 0.0 copy-start.3
  160.0 1.7 %reshape.24 = bf16[2,128,384]{2,1,0:T(8,128)(2,1)} reshape(bf16[2,64,768]{2,1,0:T(8,128)(2,1)} %get-tuple-element.6) | data formatting | bytes 393216 | tf_op jit(solution)/shard_map/reshape | solution.py:649
  161.7 0.0 copy-done.3
  161.7 0.0 copy-start.2
  161.7 0.7 reshape.25
  162.5 0.2 copy-done.2
  162.7 0.7 copy.13
Async XLA Ops:
  0.6 1.1 copy-start.1
  0.6 3.6 %copy-start = (bf16[5,96,768]{2,1,0:T(8,128)(2,1)S(1)}, bf16[5,96,768]{2,1,0:T(8,128)(2,1)}, u32[]{:S(2)}) copy-start(bf16[5,96,768]{2,1,0:T(8,128)(2,1)} %param.12) | copy-start | bytes 2211844
  2.5 1.7 %copy-start.4 = (bf16[768,96]{0,1:T(8,128)(2,1)S(1)}, bf16[768,96]{0,1:T(8,128)(2,1)}, u32[]{:S(2)}) copy-start(bf16[768,96]{0,1:T(8,128)(2,1)} %param.10) | copy-start | bytes 442372
  160.0 1.7 %copy-start.3 = (bf16[2,64,768]{2,1,0:T(8,128)(2,1)S(1)}, bf16[2,64,768]{2,1,0:T(8,128)(2,1)}, u32[]{:S(2)}) copy-start(bf16[2,64,768]{2,1,0:T(8,128)(2,1)} %get-tuple-element.7) | copy-start | bytes 589828
  161.7 1.0 copy-start.2
